TPU v7x, 32 devices: a whole 2x2x4 slice. The times are simulated.
32 devices in a mesh: grp: 4 (over y, x), docs: 8 (over z, core).
Axes of the slice: x: 2, y: 2, z: 4, core: 2. Of those that a mesh axis runs over, the one named last changes fastest.
Arguments:
- embeddings: float32 [131072, 1024], P(('grp', 'docs'))
- assign: int32 [131072], P(('grp', 'docs')), may hold values from 0 to 767, as said below
- cluster_slot: int32 [768], replicated, may hold values from 0 to 767, as said below
Outputs:
- centroids: float32 [768, 1024], P('docs')
- max_sim: float32 [131072], P(('grp', 'docs'))
- centroid_cos: float32 [131072], P(('grp', 'docs'))
Inputs may be any that keep to these rules, and one draw needn't show every extreme that they name: Each device's rows are ordered by owner, cluster_slot[assign] // 96; a device sends at most 640 rows to one owner and some device sends exactly 640; every owner receives exactly 4096 rows from the devices of its group; in each group every cluster is named by 2 to 128 rows, and some cluster by exactly 128. A permutation: cluster c is held at slot cluster_slot[c] by the owner of index cluster_slot[c] // 96 along docs.
All inputs are finite; a program needn't handle non-finite values.
Results may differ from a plain program's by a relative error of at most 0.0003.
Values may be sent and summed in bfloat16 or wider, within the bound.
No kernel may reach another device: no remote copies, remote signals or barrier semaphores. Data moves between devices by JAX's collectives and lax.ppermute only.
A program may use at most 192 MiB of HBM per device.

v0:
```python
import functools

import jax
import jax.numpy as jnp
from jax import lax
from jax.experimental import pallas as pl
from jax.experimental.pallas import tpu as pltpu
from jax.sharding import PartitionSpec as P

epsilon = 1e-06
LANES = 128
SUBLANES = 8
MIB = 1024 * 1024
TILE = 256
in_vmem = pl.BlockSpec(memory_space=pltpu.VMEM)
in_smem = pl.BlockSpec(memory_space=pltpu.SMEM)
anywhere = pl.BlockSpec(memory_space=pl.ANY)
brief = pl.CostEstimate(flops=1000, bytes_accessed=1000, transcendentals=0)


def round_up(value, step):
    return -(-value // step) * step


def params(mib=46):
    return pltpu.CompilerParams(vmem_limit_bytes=mib * MIB)


def look_up(table_ref, index):
    lane = jnp.bitwise_and(index, LANES - 1)
    row = jnp.right_shift(index, 7)
    found = jnp.zeros(index.shape, jnp.int32)
    for part in range(table_ref.shape[0]):
        entries = jnp.broadcast_to(table_ref[part : part + 1, :], index.shape)
        found = jnp.where(row == part, jnp.take_along_axis(entries, lane, axis=1), found)
    return found


def rows_below(slots, bound):
    return jnp.sum((slots < bound).astype(jnp.float32)).astype(jnp.int32)


def plan_kernel(per_owner, limit, assign_ref, table_ref, slot_ref, start_ref):
    slots = look_up(table_ref, assign_ref[...])
    slot_ref[...] = slots
    for owner in range(start_ref.shape[0]):
        start_ref[owner] = jnp.minimum(rows_below(slots, owner * per_owner), limit)


def make_plan(assign_rows, table, owner_count, per_owner, limit):
    return pl.pallas_call(
        functools.partial(plan_kernel, per_owner, limit),
        out_shape=(
            jax.ShapeDtypeStruct(assign_rows.shape, jnp.int32),
            jax.ShapeDtypeStruct((owner_count,), jnp.int32),
        ),
        in_specs=[in_vmem, in_vmem],
        out_specs=(in_vmem, in_smem),
        compiler_params=params(),
        name="plan",
    )(assign_rows, table)


def unit_kernel(steps, offset, turn, start_ref, me_ref, rows_ref, *refs):
    unit_ref, held, sem = refs[-3:]
    part = unit_ref.shape[0] // steps
    window = part + SUBLANES
    start = start_ref[lax.rem(me_ref[0] + turn, start_ref.shape[0])] + offset

    def first(step):
        return aligned_start(start + step * part, rows_ref.shape[0], window)

    copies = [
        pltpu.make_async_copy(rows_ref.at[pl.ds(first(step), window), :], held.at[step], sem.at[step])
        for step in range(steps)
    ]
    for copy in copies:
        copy.start()
    for step in range(steps):
        copies[step].wait()
        shift = start + step * part - first(step)
        groups = held[step].reshape(window // SUBLANES, SUBLANES, -1)
        turned = pltpu.roll(groups, SUBLANES - shift, 1)
        line = lax.broadcasted_iota(jnp.int32, (part // SUBLANES, SUBLANES, groups.shape[2]), 1)
        values = jnp.where(line < SUBLANES - shift, turned[:-1], turned[1:]).reshape(part, -1)
        scale = lax.rsqrt(jnp.sum(values * values, -1, keepdims=True) + epsilon)
        unit_ref[step * part : (step + 1) * part, :] = (values * scale).astype(jnp.bfloat16)


def unit_piece(starts, me, embeddings, turn, offset, rows, after):
    width = embeddings.shape[1]
    steps = rows // LANES if rows % LANES == 0 else 1
    return pl.pallas_call(
        functools.partial(unit_kernel, steps, offset, turn),
        out_shape=jax.ShapeDtypeStruct((rows, width), jnp.bfloat16),
        in_specs=[in_smem, in_smem, anywhere] + [anywhere] * len(after),
        out_specs=in_vmem,
        scratch_shapes=[
            pltpu.VMEM((steps, rows // steps + SUBLANES, width), jnp.float32),
            pltpu.SemaphoreType.DMA((steps,)),
        ],
        compiler_params=params(),
        cost_estimate=brief,
        name="unit",
    )(starts, me, embeddings, *after)


def hold_until(values, arrived):
    def nothing(*refs):
        pass

    return pl.pallas_call(
        nothing,
        out_shape=jax.ShapeDtypeStruct(values.shape, values.dtype),
        in_specs=[anywhere] * (1 + len(arrived)),
        out_specs=anywhere,
        input_output_aliases={0: 0},
        compiler_params=params(),
        name="hold",
    )(values, *arrived)


def aligned_start(start, row_count, window):
    begin = jnp.minimum(jnp.left_shift(jnp.right_shift(start, 3), 3), row_count - window)
    return pl.multiple_of(begin, SUBLANES)


def flat_window(held, start, rows):
    span = round_up(rows + 1, SUBLANES)
    shift = jnp.bitwise_and(start, LANES - 1)
    block = held[pl.ds(jnp.right_shift(start, 7), span), :]
    turned = pltpu.roll(block, jnp.bitwise_and(LANES - shift, LANES - 1), 1)
    following = pltpu.roll(turned, span - 1, 0)
    lane = lax.broadcasted_iota(jnp.int32, block.shape, 1)
    return jnp.where(lane < LANES - shift, turned, following)


def window_labels(held, slots, owner, start, per_owner, capacity, blocks):
    low = owner * per_owner
    mine = (slots >= low) & (slots < low + per_owner)
    held[: slots.shape[0], :] = jnp.where(mine, slots - low, -1)
    labels = flat_window(held, start, blocks)
    place = lax.broadcasted_iota(jnp.int32, labels.shape, 0) * LANES + lax.broadcasted_iota(
        jnp.int32, labels.shape, 1
    )
    return jnp.where(place < capacity, labels, -1)


def sent_kernel(per_owner, capacity, start_ref, slot_ref, sum_ref, sent_ref, held):
    owner_count, span, _ = sent_ref.shape
    held[...] = jnp.full(held.shape, -1, jnp.int32)
    slots = slot_ref[...]
    window = capacity + SUBLANES
    wide = sum_ref.shape[1] // LANES
    for owner in range(owner_count):
        labels = window_labels(held, slots, owner, start_ref[owner], per_owner, capacity, span - 1)
        sent_ref[owner] = labels[:span, :]
        aligned = aligned_start(start_ref[owner], slots.size, window)
        labels = window_labels(held, slots, owner, aligned, per_owner, window, wide)
        for block in range(wide):
            sum_ref[owner : owner + 1, block * LANES : (block + 1) * LANES] = labels[block : block + 1, :]


def sent_labels(starts, slots, owner_count, per_owner, capacity):
    span = round_up(-(-capacity // LANES) + 1, SUBLANES)
    return pl.pallas_call(
        functools.partial(sent_kernel, per_owner, capacity),
        out_shape=(
            jax.ShapeDtypeStruct((owner_count, round_up(capacity + SUBLANES, LANES)), jnp.int32),
            jax.ShapeDtypeStruct((owner_count, span, LANES), jnp.int32),
        ),
        in_specs=[in_smem, in_vmem],
        out_specs=(in_vmem, in_vmem),
        scratch_shapes=[pltpu.VMEM((slots.shape[0] + 2 * SUBLANES, LANES), jnp.int32)],
        compiler_params=params(),
        name="sent",
    )(starts, slots)


def arrived_kernel(blocks, turns_of, me_ref, got_ref, row_ref, column_ref, tally_ref):
    tally = jnp.zeros((LANES, LANES), jnp.float32)
    cluster = lax.broadcasted_iota(jnp.int32, tally.shape, 0)
    for place, turn in enumerate(turns_of):
        source = lax.rem(me_ref[0] + len(turns_of) - turn, len(turns_of))
        for block in range(blocks):
            line = place * blocks + block
            spread = jnp.broadcast_to(got_ref[source, block : block + 1, :], tally.shape)
            row_ref[line : line + 1, :] = spread[:1, :]
            column_ref[line * LANES : (line + 1) * LANES, :] = spread.T
            tally += (spread == cluster).astype(jnp.float32)
    total = jnp.broadcast_to(jnp.sum(tally, 1, keepdims=True), tally.shape)
    tally_ref[...] = jnp.zeros(tally_ref.shape, jnp.float32)
    tally_ref[:, :LANES] = total.T[:SUBLANES, :]


def arrived_labels(me, got, turns_of, blocks, width):
    lines = len(turns_of) * blocks
    return pl.pallas_call(
        functools.partial(arrived_kernel, blocks, turns_of),
        out_shape=(
            jax.ShapeDtypeStruct((lines, LANES), jnp.int32),
            jax.ShapeDtypeStruct((lines * LANES, LANES), jnp.int32),
            jax.ShapeDtypeStruct((SUBLANES, width), jnp.float32),
        ),
        in_specs=[in_smem, in_vmem],
        out_specs=(in_vmem, in_vmem, in_vmem),
        compiler_params=params(),
        name="arrived",
    )(me, got)


def sum_kernel(start_ref, label_ref, rows_ref, *refs):
    sum_ref, held, sem = refs[-3:]
    owner_count, per_owner, _ = sum_ref.shape
    window = held.shape[1]

    def copy(owner, slot):
        first = aligned_start(start_ref[owner], rows_ref.shape[0], window)
        return pltpu.make_async_copy(rows_ref.at[pl.ds(first, window), :], held.at[slot], sem.at[slot])

    copy(0, 0).start()

    def body(owner, carry):
        slot = lax.rem(owner, 2)

        @pl.when(owner + 1 < owner_count)
        def _():
            copy(owner + 1, 1 - slot).start()

        copy(owner, slot).wait()
        labels = label_ref[pl.ds(owner, 1), :][:, :window]
        cluster = lax.broadcasted_iota(jnp.int32, (per_owner, window), 0)
        member = (labels == cluster).astype(jnp.float32).astype(jnp.bfloat16)
        values = held[slot]
        high = values.astype(jnp.bfloat16)
        rest = values - high.astype(jnp.float32)
        middle = rest.astype(jnp.bfloat16)
        low = (rest - middle.astype(jnp.float32)).astype(jnp.bfloat16)
        total = jnp.dot(member, high, preferred_element_type=jnp.float32)
        total += jnp.dot(member, middle, preferred_element_type=jnp.float32)
        total += jnp.dot(member, low, preferred_element_type=jnp.float32)
        sum_ref[pl.ds(owner, 1)] = total[None]
        return carry

    lax.fori_loop(0, owner_count, body, 0)


def slot_sums(starts, labels, embeddings, per_owner, capacity, after):
    owner_count = labels.shape[0]
    width = embeddings.shape[1]
    return pl.pallas_call(
        sum_kernel,
        out_shape=jax.ShapeDtypeStruct((owner_count, per_owner, width), jnp.float32),
        in_specs=[in_smem, in_vmem, anywhere] + [anywhere] * len(after),
        out_specs=in_vmem,
        scratch_shapes=[
            pltpu.VMEM((2, capacity + SUBLANES, width), jnp.float32),
            pltpu.SemaphoreType.DMA((2,)),
        ],
        compiler_params=params(),
        cost_estimate=pl.CostEstimate(
            flops=6 * owner_count * per_owner * capacity * width,
            bytes_accessed=4 * embeddings.size,
            transcendentals=0,
        ),
        name="sums",
    )(starts, labels, embeddings, *after)


def gram_kernel(begin, rows, wide, after_count, turns_of, *refs):
    chunk_ref, row_ref, column_ref, best_ref, *refs = refs
    flat_ref = centroid_ref = result_ref = None
    if begin:
        flat_ref, *refs = refs
    refs = refs[after_count:]
    if turns_of:
        centroid_ref, me_ref, result_ref, *refs, out_ref, cosine_ref = refs
    else:
        out_ref, flat_ref, *refs = refs
    mine, labels, tiles, even, odd, best, sem, tile_sem = refs
    first = begin // LANES
    count = round_up(-(-begin // TILE), 2)

    def line_of(tile):
        return jnp.minimum(tile * (TILE // LANES), first - TILE // LANES)

    def fetch(tile):
        start = pl.multiple_of(line_of(tile) * LANES, LANES)
        slot = lax.rem(tile, 4)
        return pltpu.make_async_copy(flat_ref.at[pl.ds(start, TILE), :], tiles.at[slot], tile_sem.at[slot])

    chunk_copy = pltpu.make_async_copy(chunk_ref, mine.at[pl.ds(0, rows), :], sem.at[0])
    label_copy = pltpu.make_async_copy(column_ref.at[pl.ds(begin, wide), :], labels, sem.at[1])
    chunk_copy.start()
    label_copy.start()
    for tile in range(min(count, 3)):
        fetch(jnp.int32(tile)).start()
    if rows < wide:
        mine[rows:wide, :] = jnp.zeros((wide - rows, mine.shape[1]), mine.dtype)
    if turns_of:
        mine[wide:, :] = centroid_ref[...]
        cosine_ref[...] = jnp.zeros(cosine_ref.shape, jnp.float32)
    out_ref[...] = best_ref[...]
    best[...] = jnp.full(best.shape, -2.0, jnp.float32)
    chunk_copy.wait()
    label_copy.wait()
    if not turns_of:
        flat_copy = pltpu.make_async_copy(
            mine.at[pl.ds(0, wide), :], flat_ref.at[pl.ds(begin, wide), :], sem.at[2]
        )
        flat_copy.start()

    def products(right):
        return lax.dot_general(mine[...], right, (((1,), (1,)), ((), ())), preferred_element_type=jnp.float32)

    def cosines(values, line):
        cluster = lax.broadcasted_iota(jnp.int32, values.shape, 0)
        own = jnp.where(row_ref[pl.ds(line, 1), :] == cluster, values, 0.0)
        cosine_ref[pl.ds(line, 1), :] = jnp.sum(own, 0, keepdims=True)

    def reduce_tile(held, tile):
        for part in range(TILE // LANES):
            line = line_of(tile) + part
            here = slice(part * LANES, (part + 1) * LANES)
            near = jnp.where(labels[...] == row_ref[pl.ds(line, 1), :], held[:wide, here], -2.0)
            out_ref[pl.ds(line, 1), :] = jnp.maximum(
                out_ref[pl.ds(line, 1), :], jnp.max(near, 0, keepdims=True)
            )
            best[...] = jnp.maximum(best[...], near)
            if turns_of:
                cosines(held[wide:, here], line)

    if begin:
        fetch(jnp.int32(0)).wait()
        even[...] = products(tiles[0])

        def body(pair, carry):
            tile = pair * 2
            fetch(tile + 1).wait()
            fetch(tile + 3).start()
            odd[...] = products(tiles[lax.rem(tile + 1, 4)])
            reduce_tile(even, tile)
            fetch(tile + 2).wait()

            @pl.when(tile + 4 < count)
            def _():
                fetch(tile + 4).start()

            even[...] = products(tiles[lax.rem(tile + 2, 4)])
            reduce_tile(odd, tile + 1)
            return carry

        lax.fori_loop(0, count // 2 - 1, body, 0)
        fetch(jnp.int32(count - 1)).wait()
        odd[...] = products(tiles[(count - 1) % 4])
        reduce_tile(even, jnp.int32(count - 2))
        reduce_tile(odd, jnp.int32(count - 1))
    own = products(mine[:wide, :])
    row = lax.broadcasted_iota(jnp.int32, (wide, LANES), 0)
    column = lax.broadcasted_iota(jnp.int32, (wide, LANES), 1)
    for block in range(wide // LANES):
        line = first + block
        here = slice(block * LANES, (block + 1) * LANES)
        allowed = (labels[...] == row_ref[line : line + 1, :]) & (row != column + block * LANES)
        near = jnp.max(jnp.where(allowed, own[:wide, here], -2.0), 0, keepdims=True)
        other = jnp.max(best[here, :].T, 0, keepdims=True)
        out_ref[line : line + 1, :] = jnp.maximum(near, other)
        if turns_of:
            cosines(own[wide:, here], line)
    if turns_of:
        blocks = row_ref.shape[0] // len(turns_of)
        half = result_ref.shape[1] // 2
        result_ref[...] = jnp.zeros(result_ref.shape, jnp.float32)
        for place, turn in enumerate(turns_of):
            source = lax.rem(me_ref[0] + len(turns_of) - turn, len(turns_of))
            lines = slice(place * blocks, (place + 1) * blocks)
            result_ref[source, :blocks, :] = out_ref[lines, :]
            result_ref[source, half : half + blocks, :] = cosine_ref[lines, :]
    else:
        flat_copy.wait()


def gram_step(rows, columns, best, flat, chunk, begin, after=(), final=None):
    length, width = chunk.shape
    wide = round_up(length, LANES)
    tall = wide
    flat_shape = jax.ShapeDtypeStruct((columns.shape[0], width), jnp.bfloat16)
    inputs = [chunk, rows, columns, best]
    in_specs = [anywhere, in_vmem, anywhere, in_vmem]
    aliases = {}
    if begin:
        if not final:
            aliases = {len(inputs): 1}
        inputs.append(flat)
        in_specs.append(anywhere)
    inputs += after
    in_specs += [anywhere] * len(after)
    out_shape = (jax.ShapeDtypeStruct(best.shape, jnp.float32), flat_shape)
    out_specs = (in_vmem, anywhere)
    turns_of = ()
    extra = []
    if final:
        centroid_unit, me, turns_of = final
        tall += centroid_unit.shape[0]
        inputs += [centroid_unit, me]
        in_specs += [in_vmem, in_smem]
        half = round_up(rows.shape[0] // len(turns_of) + 1, SUBLANES)
        out_shape = jax.ShapeDtypeStruct((len(turns_of), 2 * half, LANES), jnp.float32)
        out_specs = in_vmem
        extra = [pltpu.VMEM(best.shape, jnp.float32)] * 2
    return pl.pallas_call(
        functools.partial(gram_kernel, begin, length, wide, len(after), turns_of),
        out_shape=out_shape,
        in_specs=in_specs,
        out_specs=out_specs,
        scratch_shapes=[
            pltpu.VMEM((tall, width), jnp.bfloat16),
            pltpu.VMEM((wide, LANES), jnp.int32),
            pltpu.VMEM((4, TILE, width), jnp.bfloat16),
            pltpu.VMEM((tall, TILE), jnp.float32),
            pltpu.VMEM((tall, TILE), jnp.float32),
            pltpu.VMEM((wide, LANES), jnp.float32),
            pltpu.SemaphoreType.DMA((3,)),
            pltpu.SemaphoreType.DMA((4,)),
        ]
        + extra,
        input_output_aliases=aliases,
        compiler_params=params(),
        cost_estimate=brief,
        name="gram",
    )(*inputs)


def pack_kernel(share_ref, tally_ref, *refs):
    packed_ref = refs[-1]
    packed_ref[: share_ref.shape[0], :] = share_ref[...]
    packed_ref[share_ref.shape[0] :, :] = tally_ref[...]


def pack_share(share, tally, after):
    length = share.shape[0] + tally.shape[0]
    return pl.pallas_call(
        pack_kernel,
        out_shape=jax.ShapeDtypeStruct((length, share.shape[1]), jnp.float32),
        in_specs=[in_vmem, in_vmem] + [anywhere] * len(after),
        out_specs=in_vmem,
        compiler_params=params(),
        name="pack",
    )(share, tally, *after)


def centroid_kernel(gathered_ref, centroid_ref, unit_ref):
    groups, length, width = gathered_ref.shape
    share = length - SUBLANES
    per_owner = centroid_ref.shape[0]
    tally = jnp.sum(gathered_ref[:, share, :LANES], 0, keepdims=True)
    column = jnp.broadcast_to(tally, (LANES, LANES)).T[:per_owner, :]
    sums = jnp.concatenate([gathered_ref[group, :share, :] for group in range(groups)], 0)
    centroids = sums / jnp.concatenate([column] * (width // LANES), 1)
    centroid_ref[...] = centroids
    scale = lax.rsqrt(jnp.sum(centroids * centroids, -1, keepdims=True) + epsilon)
    unit_ref[...] = (centroids * scale).astype(jnp.bfloat16)


def make_centroids(gathered, per_owner):
    shape = (per_owner, gathered.shape[2])
    return pl.pallas_call(
        centroid_kernel,
        out_shape=(
            jax.ShapeDtypeStruct(shape, jnp.float32),
            jax.ShapeDtypeStruct(shape, jnp.bfloat16),
        ),
        in_specs=[in_vmem],
        out_specs=(in_vmem, in_vmem),
        compiler_params=params(),
        name="centroids",
    )(gathered)


def place_kernel(per_owner, start_ref, slot_ref, back_ref, near_ref, cosine_ref, held, result):
    owner_count, double, _ = back_ref.shape
    span = double // 2
    rows = slot_ref.shape[0]
    held[...] = jnp.full(held.shape, -1, jnp.int32)
    held[:rows, :] = slot_ref[...]
    result[...] = jnp.zeros(result.shape, jnp.float32)
    lane = lax.broadcasted_iota(jnp.int32, (span, LANES), 1)
    for owner in range(owner_count):
        start = start_ref[owner]
        first = pl.ds(jnp.right_shift(start, 7), span)
        shift = jnp.bitwise_and(start, LANES - 1)
        slots = held[first, :]
        mine = (slots >= owner * per_owner) & (slots < (owner + 1) * per_owner)
        for kind in range(2):
            turned = pltpu.roll(back_ref[owner, kind * span : (kind + 1) * span, :], shift, 1)
            earlier = pltpu.roll(turned, 1, 0)
            moved = jnp.where(lane >= shift, turned, earlier)
            result[kind, first, :] = jnp.where(mine, moved, result[kind, first, :])
    near_ref[...] = result[0, :rows, :]
    cosine_ref[...] = result[1, :rows, :]


def place_rows(starts, slots, back, per_owner):
    span = back.shape[1] // 2
    rows = slots.shape[0]
    return pl.pallas_call(
        functools.partial(place_kernel, per_owner),
        out_shape=(jax.ShapeDtypeStruct(slots.shape, jnp.float32),) * 2,
        in_specs=[in_smem, in_vmem, in_vmem],
        out_specs=(in_vmem, in_vmem),
        scratch_shapes=[
            pltpu.VMEM((rows + span, LANES), jnp.int32),
            pltpu.VMEM((2, rows + span, LANES), jnp.float32),
        ],
        compiler_params=params(),
        name="place",
    )(starts, slots, back)


def turns(count):
    order = sorted(range(count), key=lambda turn: (min(turn, count - turn), turn))
    return order[:1] + order[3:4] + order[1:3] + order[4:]


IN_FLIGHT = 2


def per_device(embeddings, assign, cluster_slot):
    row_count, width = embeddings.shape
    owner_count = lax.axis_size("docs")
    per_owner = cluster_slot.shape[0] // owner_count
    capacity = row_count // owner_count + row_count // (4 * owner_count)
    padded = round_up(capacity, LANES)
    blocks = padded // LANES
    me = lax.axis_index("docs").astype(jnp.int32).reshape(1)
    turns_of = turns(owner_count)

    pieces = []
    for place, turn in enumerate(turns_of):
        if capacity < padded or blocks < 5 or place < owner_count - 3:
            cuts = [0, capacity]
        elif place < owner_count - 1:
            cuts = [0, 3 * LANES, capacity]
        else:
            cuts = [0, 2 * LANES, 4 * LANES, capacity]
        for low, high in zip(cuts, cuts[1:]):
            pieces.append((turn, low, high - low, place * padded + low))

    slots, starts = make_plan(
        assign.reshape(-1, LANES), cluster_slot.reshape(-1, LANES), owner_count, per_owner, row_count - capacity
    )
    sum_labels, wire_labels = sent_labels(starts, slots, owner_count, per_owner, capacity)
    got_labels = lax.all_to_all(wire_labels, "docs", split_axis=0, concat_axis=0, tiled=True)
    rows, columns, group_tally = arrived_labels(me, got_labels, turns_of, blocks, width)

    chunks, sent = [], []
    bests = [jnp.full((owner_count * blocks, LANES), -2.0, jnp.float32)]
    flat = group_share = share = None

    def multiply(index):
        after = [group_share] if index == len(pieces) // 4 else []
        best, held = gram_step(rows, columns, bests[-1], flat, chunks[index], pieces[index][3], after)
        bests.append(best)
        return held

    for index, (turn, offset, length, _) in enumerate(pieces):
        after = [got_labels] if index == IN_FLIGHT else []
        if index > IN_FLIGHT:
            after += [chunks[index - IN_FLIGHT - (index == len(pieces) - 1)], sent[-1]]
        if index > IN_FLIGHT + 2:
            flat = multiply(index - IN_FLIGHT - 3)
            after.append(bests[-1])
        piece = unit_piece(starts, me, embeddings, turn, offset, length, after)
        sent.append(piece)
        if turn:
            piece = lax.ppermute(piece, "docs", [(i, (i + turn) % owner_count) for i in range(owner_count)])
        chunks.append(piece)
        if index == IN_FLIGHT + 1:
            partial_sums = slot_sums(starts, sum_labels, embeddings, per_owner, capacity, sent[: IN_FLIGHT + 1])
            partial_sums = hold_until(partial_sums, chunks[1 : IN_FLIGHT + 1] + sent[IN_FLIGHT + 1 :])
            group_share = lax.psum_scatter(partial_sums, "grp", scatter_dimension=1, tiled=True)
            share = lax.psum_scatter(group_share, "docs", scatter_dimension=0, tiled=True)[0]
    for index in range(len(bests) - 1, len(pieces) - 1):
        flat = multiply(index)
    packed = pack_share(share, group_tally, [bests[-2], sent[-1]])
    centroids, centroid_unit = make_centroids(lax.all_gather(packed, "grp"), per_owner)
    results = gram_step(
        rows, columns, bests[-1], flat, chunks[-1], pieces[-1][3], final=(centroid_unit, me, turns_of)
    )
    back = lax.all_to_all(results, "docs", split_axis=0, concat_axis=0, tiled=True)
    near, cosine = place_rows(starts, slots, back, per_owner)
    return (centroids, near.reshape(-1), cosine.reshape(-1))


def solution(mesh):
    placed = (P(("grp", "docs"), None), P(("grp", "docs")), P())
    return jax.shard_map(
        per_device,
        mesh=mesh,
        in_specs=placed,
        out_specs=(P("docs", None), P(("grp", "docs")), P(("grp", "docs"))),
        check_vma=False,
    )
```

profile of v0, /device:TPU:0, one launch (start us, length us, event | category | flops | bytes accessed | tf_op | source)
XLA Modules:
  0.0 344.1 jit_solution(17736941740671528440)
XLA Ops:
  10.8 6.3 %all-to-all-start = ((s32[8,8,128]{2,1,0:T(8,128)}), s32[8,8,128]{2,1,0:T(8,128)S(1)}, u32[]{:S(2)}, u32[]{:S(2)}) async-start(s32[8,8,128]{2,1,0:T(8,128)} %get-tuple-element.39), calls=%async_computation | async-start | bytes 65536 | tf_op jit(solution)/shard_map/all_to_all | solution.py:553
  17.1 3.5 %unit.13.refs_1_ = bf16[640,1024]{1,0:T(8,128)(2,1)} custom-call(s32[8]{0:T(128)S(1)} %get-tuple-element.36.start_ref, s32[1]{0:T(128)} %bitcast.2.me_ref.refs_6_, f32[4096,1024]{1,0:T(8,128)} %rows_ref.25), custom_call_target="tpu_custom_call" | custom-call | flops 1000 | bytes 1000 | tf_op jit(solution)/shard_map/unit/pallas_call | solution.py:93
  27.9 15.0 %sums.1.refs_0_ = f32[8,96,1024]{2,1,0:T(8,128)} custom-call(s32[8]{0:T(128)S(1)} %get-tuple-element.36.start_ref, s32[8,768]{1,0:T(8,128)S(1)} %get-tuple-element.38.label_ref, f32[4096,1024]{1,0:T(8,128)} %rows_ref.25, bf16[640,1024]{1,0:T(8,128)(2,1)S(1)} %unit.12.refs_0_, bf16[640,1024]{1,0:T(8,128)(2,1)} %unit.13.refs_1_, ...), custom_call_target="tpu_custom_call" | custom-call | flops 3019898880 | bytes 16777216 | tf_op jit(solution)/shard_map/sums/pallas_call | solution.py:251
  42.9 11.4 %collective-permute-done.refs_0_.refs_1_ = bf16[640,1024]{1,0:T(8,128)(2,1)S(1)} collective-permute-done((bf16[640,1024]{1,0:T(8,128)(2,1)}, bf16[640,1024]{1,0:T(8,128)(2,1)S(1)}, u32[]{:S(2)}, u32[]{:S(2)}) %collective-permute-start) | collective-permute-done | bytes 1310752 | tf_op jit(solution)/shard_map/ppermute | solution.py:576
  56.8 11.1 %collective-permute-done.1.refs_2_.refs_0_ = bf16[640,1024]{1,0:T(8,128)(2,1)S(1)} collective-permute-done((bf16[640,1024]{1,0:T(8,128)(2,1)S(1)}, bf16[640,1024]{1,0:T(8,128)(2,1)S(1)}, u32[]{:S(2)}, u32[]{:S(2)}) %collective-permute-start.1) | collective-permute-done | bytes 1310752 | tf_op jit(solution)/shard_map/ppermute | solution.py:576
  77.3 16.4 %collective-permute-done.2.refs_0_ = bf16[640,1024]{1,0:T(8,128)(2,1)S(1)} collective-permute-done((bf16[640,1024]{1,0:T(8,128)(2,1)}, bf16[640,1024]{1,0:T(8,128)(2,1)S(1)}, u32[]{:S(2)}, u32[]{:S(2)}) %collective-permute-start.2) | collective-permute-done | bytes 1310752 | tf_op jit(solution)/shard_map/ppermute | solution.py:576
  98.1 5.7 %gram.13 = (f32[40,128]{1,0:T(8,128)S(1)}, bf16[5120,1024]{1,0:T(8,128)(2,1)}) custom-call(bf16[640,1024]{1,0:T(8,128)(2,1)S(1)} %copy-done.5, s32[40,128]{1,0:T(8,128)S(1)} %get-tuple-element.41.refs_1_, s32[5120,128]{1,0:T(8,128)S(1)} %get-tuple-element.42.refs_2_, ...), custom_call_target="tpu_custom_call", output_to_operand_aliasing={{1}: (4, {})} | custom-call | flops 1000 | bytes 1000 | tf_op jit(solution)/shard_map/gram/pallas_call | solution.py:411
  103.8 17.3 %collective-permute-done.4.refs_0_ = bf16[640,1024]{1,0:T(8,128)(2,1)S(1)} collective-permute-done((bf16[640,1024]{1,0:T(8,128)(2,1)S(1)}, bf16[640,1024]{1,0:T(8,128)(2,1)S(1)}, u32[]{:S(2)}, u32[]{:S(2)}) %collective-permute-start.4) | collective-permute-done | bytes 1310752 | tf_op jit(solution)/shard_map/ppermute | solution.py:576
  126.3 7.5 %gram.14 = (f32[40,128]{1,0:T(8,128)S(1)}, bf16[5120,1024]{1,0:T(8,128)(2,1)}) custom-call(bf16[640,1024]{1,0:T(8,128)(2,1)S(1)} %copy-done.3, s32[40,128]{1,0:T(8,128)S(1)} %get-tuple-element.41.refs_1_, s32[5120,128]{1,0:T(8,128)S(1)} %get-tuple-element.42.refs_2_, ...), custom_call_target="tpu_custom_call", output_to_operand_aliasing={{1}: (4, {})} | custom-call | flops 1000 | bytes 1000 | tf_op jit(solution)/shard_map/gram/pallas_call | solution.py:411
  133.8 9.2 %collective-permute-done.3.refs_0_ = bf16[384,1024]{1,0:T(8,128)(2,1)} collective-permute-done((bf16[384,1024]{1,0:T(8,128)(2,1)S(1)}, bf16[384,1024]{1,0:T(8,128)(2,1)}, u32[]{:S(2)}, u32[]{:S(2)}) %collective-permute-start.3) | collective-permute-done | bytes 786464 | tf_op jit(solution)/shard_map/ppermute | solution.py:576
  145.3 9.4 %gram.15 = (f32[40,128]{1,0:T(8,128)S(1)}, bf16[5120,1024]{1,0:T(8,128)(2,1)}) custom-call(bf16[640,1024]{1,0:T(8,128)(2,1)S(1)} %copy-done.9, s32[40,128]{1,0:T(8,128)S(1)} %get-tuple-element.41.refs_1_, s32[5120,128]{1,0:T(8,128)S(1)} %get-tuple-element.42.refs_2_, ...), custom_call_target="tpu_custom_call", output_to_operand_aliasing={{1}: (4, {})} | custom-call | flops 1000 | bytes 1000 | tf_op jit(solution)/shard_map/gram/pallas_call | solution.py:411
  154.6 4.3 %collective-permute-done.6.refs_0_ = bf16[256,1024]{1,0:T(8,128)(2,1)} collective-permute-done((bf16[256,1024]{1,0:T(8,128)(2,1)}, bf16[256,1024]{1,0:T(8,128)(2,1)}, u32[]{:S(2)}, u32[]{:S(2)}) %collective-permute-start.6) | collective-permute-done | bytes 524320 | tf_op jit(solution)/shard_map/ppermute | solution.py:576
  160.9 34.1 %collective-permute-start.8 = (bf16[256,1024]{1,0:T(8,128)(2,1)S(1)}, bf16[256,1024]{1,0:T(8,128)(2,1)S(1)}, u32[]{:S(2)}, u32[]{:S(2)}) collective-permute-start(bf16[256,1024]{1,0:T(8,128)(2,1)S(1)} %unit.20.refs_1_), channel_id=1, source_target_pairs={{0,5},{1,6},{2,7},{3,0},{4,1},{5,2},{6,3},{7,4},{8,13},{9,14},{10,... | collective-permute-start | bytes 1572872 | tf_op jit(solution)/shard_map/ppermute | solution.py:576
  195.0 11.2 %gram.16 = (f32[40,128]{1,0:T(8,128)S(1)}, bf16[5120,1024]{1,0:T(8,128)(2,1)}) custom-call(bf16[640,1024]{1,0:T(8,128)(2,1)S(1)} %copy-done.11, s32[40,128]{1,0:T(8,128)S(1)} %get-tuple-element.41.refs_1_, s32[5120,128]{1,0:T(8,128)S(1)} %get-tuple-element.42.refs_2_, ...), custom_call_target="tpu_custom_call", output_to_operand_aliasing={{1}: (4, {})} | custom-call | flops 1000 | bytes 1000 | tf_op jit(solution)/shard_map/gram/pallas_call | solution.py:411
  208.3 10.7 %gram.17 = (f32[40,128]{1,0:T(8,128)S(1)}, bf16[5120,1024]{1,0:T(8,128)(2,1)}) custom-call(bf16[384,1024]{1,0:T(8,128)(2,1)} %collective-permute-done.3.refs_0_, s32[40,128]{1,0:T(8,128)S(1)} %get-tuple-element.41.refs_1_, s32[5120,128]{1,0:T(8,128)S(1)} %get-tuple-element.42.refs_2_, ...), custom_call_target="tpu_custom_call", output_to_operand_aliasing={{1}: (4, {})} | custom-call | flops 1000 | bytes 1000 | tf_op jit(solution)/shard_map/gram/pallas_call | solution.py:411
  221.0 2.9 collective-permute-start.10
  224.0 8.7 %gram.18 = (f32[40,128]{1,0:T(8,128)S(1)}, bf16[5120,1024]{1,0:T(8,128)(2,1)}) custom-call(bf16[256,1024]{1,0:T(8,128)(2,1)} %collective-permute-done.6.refs_0_, s32[40,128]{1,0:T(8,128)S(1)} %get-tuple-element.41.refs_1_, s32[5120,128]{1,0:T(8,128)S(1)} %get-tuple-element.42.refs_2_, ...), custom_call_target="tpu_custom_call", output_to_operand_aliasing={{1}: (4, {})} | custom-call | flops 1000 | bytes 1000 | tf_op jit(solution)/shard_map/gram/pallas_call | solution.py:411
  234.5 12.3 %gram.19 = (f32[40,128]{1,0:T(8,128)S(1)}, bf16[5120,1024]{1,0:T(8,128)(2,1)}) custom-call(bf16[384,1024]{1,0:T(8,128)(2,1)S(1)} %collective-permute-done.5.refs_0_, s32[40,128]{1,0:T(8,128)S(1)} %get-tuple-element.41.refs_1_, s32[5120,128]{1,0:T(8,128)S(1)} %get-tuple-element.42.refs_2_, ...), custom_call_target="tpu_custom_call", output_to_operand_aliasing={{1}: (4, {})} | custom-call | flops 1000 | bytes 1000 | tf_op jit(solution)/shard_map/gram/pallas_call | solution.py:411
  246.8 11.0 %gram.20 = (f32[40,128]{1,0:T(8,128)S(1)}, bf16[5120,1024]{1,0:T(8,128)(2,1)}) custom-call(bf16[256,1024]{1,0:T(8,128)(2,1)S(1)} %collective-permute-done.8.refs_0_, s32[40,128]{1,0:T(8,128)S(1)} %get-tuple-element.41.refs_1_, s32[5120,128]{1,0:T(8,128)S(1)} %get-tuple-element.42.refs_2_, ...), custom_call_target="tpu_custom_call", output_to_operand_aliasing={{1}: (4, {})} | custom-call | flops 1000 | bytes 1000 | tf_op jit(solution)/shard_map/gram/pallas_call | solution.py:411
  257.9 11.0 %gram.21 = (f32[40,128]{1,0:T(8,128)S(1)}, bf16[5120,1024]{1,0:T(8,128)(2,1)}) custom-call(bf16[256,1024]{1,0:T(8,128)(2,1)S(1)} %collective-permute-done.7.refs_0_, s32[40,128]{1,0:T(8,128)S(1)} %get-tuple-element.41.refs_1_, s32[5120,128]{1,0:T(8,128)S(1)} %get-tuple-element.42.refs_2_, ...), custom_call_target="tpu_custom_call", output_to_operand_aliasing={{1}: (4, {})} | custom-call | flops 1000 | bytes 1000 | tf_op jit(solution)/shard_map/gram/pallas_call | solution.py:411
  269.0 12.1 %gram.22 = (f32[40,128]{1,0:T(8,128)S(1)}, bf16[5120,1024]{1,0:T(8,128)(2,1)}) custom-call(bf16[256,1024]{1,0:T(8,128)(2,1)S(1)} %collective-permute-done.10.refs_0_, s32[40,128]{1,0:T(8,128)S(1)} %get-tuple-element.41.refs_1_, s32[5120,128]{1,0:T(8,128)S(1)} %get-tuple-element.42.refs_2_, ...), custom_call_target="tpu_custom_call", output_to_operand_aliasing={{1}: (4, {})} | custom-call | flops 1000 | bytes 1000 | tf_op jit(solution)/shard_map/gram/pallas_call | solution.py:411
  282.0 10.1 %all-gather = f32[128,1024]{1,0:T(8,128)S(1)} all-gather(f32[32,1024]{1,0:T(8,128)S(1)} %pack.1), channel_id=2, replica_groups=mesh['grp'=4,'docs'=8] {'grp'}, dimensions={0}, use_global_device_ids=true | all-gather | bytes 655360 | tf_op jit(solution)/shard_map/all_gather | solution.py:586
  293.0 11.8 %gram.23 = f32[8,16,128]{2,1,0:T(8,128)S(1)} custom-call(bf16[128,1024]{1,0:T(8,128)(2,1)} %collective-permute-done.9.refs_0_, s32[40,128]{1,0:T(8,128)S(1)} %get-tuple-element.41.refs_1_, s32[5120,128]{1,0:T(8,128)S(1)} %get-tuple-element.42.refs_2_, f32[40,128]{1,0:T(8,128)S(1)} %get-tuple-element.64.refs_3_, ...), custom_call_target="tpu_custom_call" | custom-call | flops 1000 | bytes 1000 | tf_op jit(solution)/shard_map/gram/pallas_call | solution.py:411
  304.8 31.2 %all_to_all.10.back_ref = f32[8,16,128]{2,1,0:T(8,128)S(1)} all-to-all(f32[8,16,128]{2,1,0:T(8,128)S(1)} %gram.23), channel_id=1, replica_groups=mesh['grp'=4,'docs'=8] {'docs'}, dimensions={0} | all-to-all | bytes 131072 | tf_op jit(solution)/shard_map/all_to_all | solution.py:590
  (73 shorter events, 45.2 us)
Async XLA Ops:
  10.8 12.1 %all-to-all-start = ((s32[8,8,128]{2,1,0:T(8,128)}), s32[8,8,128]{2,1,0:T(8,128)S(1)}, u32[]{:S(2)}, u32[]{:S(2)}) async-start(s32[8,8,128]{2,1,0:T(8,128)} %get-tuple-element.39), calls=%async_computation | async-start | bytes 65536 | tf_op jit(solution)/shard_map/all_to_all | solution.py:553
  17.1 107.8 %reduce-scatter.3.cloned.1.call-start = ((), (), s32[]{:S(2)}) async-start(), calls=%async_computation.4 | async-start | bytes 3932160 | tf_op jit(solution)/shard_map/reduce_scatter | solution.py:581
  20.7 33.6 %collective-permute-start = (bf16[640,1024]{1,0:T(8,128)(2,1)}, bf16[640,1024]{1,0:T(8,128)(2,1)S(1)}, u32[]{:S(2)}, u32[]{:S(2)}) collective-permute-start(bf16[640,1024]{1,0:T(8,128)(2,1)} %unit.13.refs_1_), channel_id=1, source_target_pairs={{0,2},{1,3},{2,4},{3,5},{4,6},{5,7},{6,0},{7,1},{8,10},{9,11},{10,... | collective-permute-start | bytes 3932168 | tf_op jit(solution)/shard_map/ppermute | solution.py:576
  25.3 42.6 %collective-permute-start.1 = (bf16[640,1024]{1,0:T(8,128)(2,1)S(1)}, bf16[640,1024]{1,0:T(8,128)(2,1)S(1)}, u32[]{:S(2)}, u32[]{:S(2)}) collective-permute-start(bf16[640,1024]{1,0:T(8,128)(2,1)S(1)} %unit.14.refs_2_.refs_1_), channel_id=1, source_target_pairs={{0,1},{1,2},{2,3},{3,4},{4,5},{5,6},{6,7},{7,0},{8,9},{9,10},{10,1... | collective-permute-start | bytes 3932168 | tf_op jit(solution)/shard_map/ppermute | solution.py:576
  27.9 15.0 %copy-start = (bf16[640,1024]{1,0:T(8,128)(2,1)}, bf16[640,1024]{1,0:T(8,128)(2,1)S(1)}, u32[]{:S(2)}) copy-start(bf16[640,1024]{1,0:T(8,128)(2,1)S(1)} %unit.12.refs_0_) | copy-start | bytes 3932164
  54.3 13.6 %copy-start.4 = (bf16[640,1024]{1,0:T(8,128)(2,1)}, bf16[640,1024]{1,0:T(8,128)(2,1)S(1)}, u32[]{:S(2)}) copy-start(bf16[640,1024]{1,0:T(8,128)(2,1)S(1)} %collective-permute-done.refs_0_.refs_1_) | copy-start | bytes 3932164
  67.9 5.1 %copy-start.2 = (bf16[640,1024]{1,0:T(8,128)(2,1)}, bf16[640,1024]{1,0:T(8,128)(2,1)S(1)}, u32[]{:S(2)}) copy-start(bf16[640,1024]{1,0:T(8,128)(2,1)S(1)} %collective-permute-done.1.refs_2_.refs_0_) | copy-start | bytes 3932164
  69.0 212.1 %reduce-scatter.5.cloned.1.call-start = ((), (), s32[]{:S(2)}) async-start(), calls=%async_computation.5 | async-start | bytes 884736 | tf_op jit(solution)/shard_map/reduce_scatter | solution.py:582
  69.1 6.7 %copy-start.1 = (bf16[640,1024]{1,0:T(8,128)(2,1)S(1)}, bf16[640,1024]{1,0:T(8,128)(2,1)}, u32[]{:S(2)}) copy-start(bf16[640,1024]{1,0:T(8,128)(2,1)} %copy-done) | copy-start | bytes 3932164
  69.1 24.6 %collective-permute-start.2 = (bf16[640,1024]{1,0:T(8,128)(2,1)}, bf16[640,1024]{1,0:T(8,128)(2,1)S(1)}, u32[]{:S(2)}, u32[]{:S(2)}) collective-permute-start(bf16[640,1024]{1,0:T(8,128)(2,1)} %copy-done.6), channel_id=1, source_target_pairs={{0,7},{1,0},{2,1},{3,2},{4,3},{5,4},{6,5},{7,6},{8,15},{9,8},{10,9... | collective-permute-start | bytes 3932168 | tf_op jit(solution)/shard_map/ppermute | solution.py:576
  69.2 1.4 copy-start.7
  73.1 48.0 %collective-permute-start.4 = (bf16[640,1024]{1,0:T(8,128)(2,1)S(1)}, bf16[640,1024]{1,0:T(8,128)(2,1)S(1)}, u32[]{:S(2)}, u32[]{:S(2)}) collective-permute-start(bf16[640,1024]{1,0:T(8,128)(2,1)S(1)} %unit.16.refs_1_), channel_id=1, source_target_pairs={{0,6},{1,7},{2,0},{3,1},{4,2},{5,3},{6,4},{7,5},{8,14},{9,15},{10,... | collective-permute-start | bytes 3932168 | tf_op jit(solution)/shard_map/ppermute | solution.py:576
  77.3 20.8 %copy-start.5 = (bf16[640,1024]{1,0:T(8,128)(2,1)S(1)}, bf16[640,1024]{1,0:T(8,128)(2,1)}, u32[]{:S(2)}) copy-start(bf16[640,1024]{1,0:T(8,128)(2,1)} %copy-done.4) | copy-start | bytes 3932164
  93.7 10.1 %copy-start.8 = (bf16[640,1024]{1,0:T(8,128)(2,1)}, bf16[640,1024]{1,0:T(8,128)(2,1)S(1)}, u32[]{:S(2)}) copy-start(bf16[640,1024]{1,0:T(8,128)(2,1)S(1)} %collective-permute-done.2.refs_0_) | copy-start | bytes 3932164
  95.9 47.2 %collective-permute-start.3 = (bf16[384,1024]{1,0:T(8,128)(2,1)S(1)}, bf16[384,1024]{1,0:T(8,128)(2,1)}, u32[]{:S(2)}, u32[]{:S(2)}) collective-permute-start(bf16[384,1024]{1,0:T(8,128)(2,1)S(1)} %unit.17.refs_1_), channel_id=1, source_target_pairs={{0,3},{1,4},{2,5},{3,6},{4,7},{5,0},{6,1},{7,2},{8,11},{9,12},{10,... | collective-permute-start | bytes 2359304 | tf_op jit(solution)/shard_map/ppermute | solution.py:576
  124.9 34.0 %collective-permute-start.6 = (bf16[256,1024]{1,0:T(8,128)(2,1)}, bf16[256,1024]{1,0:T(8,128)(2,1)}, u32[]{:S(2)}, u32[]{:S(2)}) collective-permute-start(bf16[256,1024]{1,0:T(8,128)(2,1)} %unit.18.refs_1_), channel_id=1, source_target_pairs={{0,3},{1,4},{2,5},{3,6},{4,7},{5,0},{6,1},{7,2},{8,11},{9,12},{10,... | collective-permute-start | bytes 1572872 | tf_op jit(solution)/shard_map/ppermute | solution.py:576
  133.8 11.4 %copy-start.9 = (bf16[640,1024]{1,0:T(8,128)(2,1)S(1)}, bf16[640,1024]{1,0:T(8,128)(2,1)}, u32[]{:S(2)}) copy-start(bf16[640,1024]{1,0:T(8,128)(2,1)} %copy-done.8) | copy-start | bytes 3932164
  133.8 11.4 %copy-start.12 = (f32[8,24,1024]{2,1,0:T(8,128)S(1)}, f32[8,24,1024]{2,1,0:T(8,128)}, u32[]{:S(2)}) copy-start(f32[8,24,1024]{2,1,0:T(8,128)} %reduce-scatter.3.cloned.1.call-done.refs_5_) | copy-start | bytes 2359300
  145.2 61.1 %collective-permute-start.5 = (bf16[384,1024]{1,0:T(8,128)(2,1)S(1)}, bf16[384,1024]{1,0:T(8,128)(2,1)S(1)}, u32[]{:S(2)}, u32[]{:S(2)}) collective-permute-start(bf16[384,1024]{1,0:T(8,128)(2,1)S(1)} %unit.19.refs_1_), channel_id=1, source_target_pairs={{0,5},{1,6},{2,7},{3,0},{4,1},{5,2},{6,3},{7,4},{8,13},{9,14},{10,... | collective-permute-start | bytes 2359304 | tf_op jit(solution)/shard_map/ppermute | solution.py:576
  154.6 40.4 %copy-start.11 = (bf16[640,1024]{1,0:T(8,128)(2,1)S(1)}, bf16[640,1024]{1,0:T(8,128)(2,1)}, u32[]{:S(2)}) copy-start(bf16[640,1024]{1,0:T(8,128)(2,1)} %copy-done.10) | copy-start | bytes 3932164
  160.9 58.1 %collective-permute-start.8 = (bf16[256,1024]{1,0:T(8,128)(2,1)S(1)}, bf16[256,1024]{1,0:T(8,128)(2,1)S(1)}, u32[]{:S(2)}, u32[]{:S(2)}) collective-permute-start(bf16[256,1024]{1,0:T(8,128)(2,1)S(1)} %unit.20.refs_1_), channel_id=1, source_target_pairs={{0,5},{1,6},{2,7},{3,0},{4,1},{5,2},{6,3},{7,4},{8,13},{9,14},{10,... | collective-permute-start | bytes 1572872 | tf_op jit(solution)/shard_map/ppermute | solution.py:576
  208.3 49.6 %collective-permute-start.7 = (bf16[256,1024]{1,0:T(8,128)(2,1)S(1)}, bf16[256,1024]{1,0:T(8,128)(2,1)S(1)}, u32[]{:S(2)}, u32[]{:S(2)}) collective-permute-start(bf16[256,1024]{1,0:T(8,128)(2,1)S(1)} %unit.21.refs_1_), channel_id=1, source_target_pairs={{0,4},{1,5},{2,6},{3,7},{4,0},{5,1},{6,2},{7,3},{8,12},{9,13},{10,... | collective-permute-start | bytes 1572872 | tf_op jit(solution)/shard_map/ppermute | solution.py:576
  221.0 47.9 %collective-permute-start.10 = (bf16[256,1024]{1,0:T(8,128)(2,1)S(1)}, bf16[256,1024]{1,0:T(8,128)(2,1)S(1)}, u32[]{:S(2)}, u32[]{:S(2)}) collective-permute-start(bf16[256,1024]{1,0:T(8,128)(2,1)S(1)} %unit.22.refs_1_), channel_id=1, source_target_pairs={{0,4},{1,5},{2,6},{3,7},{4,0},{5,1},{6,2},{7,3},{8,12},{9,13},{10,... | collective-permute-start | bytes 1572872 | tf_op jit(solution)/shard_map/ppermute | solution.py:576
  234.4 58.6 %collective-permute-start.9 = (bf16[128,1024]{1,0:T(8,128)(2,1)S(1)}, bf16[128,1024]{1,0:T(8,128)(2,1)}, u32[]{:S(2)}, u32[]{:S(2)}) collective-permute-start(bf16[128,1024]{1,0:T(8,128)(2,1)S(1)} %unit.23.refs_1_), channel_id=1, source_target_pairs={{0,4},{1,5},{2,6},{3,7},{4,0},{5,1},{6,2},{7,3},{8,12},{9,13},{10,... | collective-permute-start | bytes 786440 | tf_op jit(solution)/shard_map/ppermute | solution.py:576
  (6 other events, 5.8 us)
Sparse Core Ops, SparseCore 0:
  69.2 43.2 reduce-scatter.2
  125.1 71.4 reduce-scatter.4
where the time goes:
time: 346 us; the launch traced here: 344 us
  Pallas kernels  161 us (47%)
  waiting for transfers between devices  70 us (20%)
  starting transfers between devices  49.8 us (14%)
  blocking collectives  41.3 us (12%)
  between operations  14.5 us (4%)
  local copies, waits for them, and re-layouts  7.18 us (2%)
    pallas_call x12, Pallas kernels, gram_step(): pl.pallas_call(functools.partial(gram_kernel, begin, length, wide, len(af...  113 us
    ppermute x11, waiting for transfers between devices, per_device(): lax.ppermute(piece, 'docs', [(i, (i + turn) % owner_count) for i in range...  69.8 us
    ppermute x11, starting transfers between devices, per_device(): lax.ppermute(piece, 'docs', [(i, (i + turn) % owner_count) for i in range...  43.4 us
    all_to_all x1, blocking collectives, per_device(): lax.all_to_all(results, 'docs', split_axis=0, concat_axis=0, tiled=True)  31.2 us
    pallas_call x12, Pallas kernels, unit_piece(): pl.pallas_call(functools.partial(unit_kernel, steps, offset, turn), out_s...  28.1 us
    pallas_call x1, Pallas kernels, slot_sums(): pl.pallas_call(sum_kernel, out_shape=jax.ShapeDtypeStruct((owner_count, p...  15 us
    all_gather x1, blocking collectives, per_device(): lax.all_gather(packed, 'grp')  10.1 us
    unnamed x32, local copies, waits for them, and re-layouts  7.18 us
  transfers between devices with their start and end apart: 14, of which 7 were waited for; matrix products, arithmetic and copies ran while one was open for 0% of the time, Pallas kernels for 42%

commit v1 on v0

--- a/solution.py
+++ b/solution.py
@@ -11,7 +11,7 @@
 LANES = 128
 SUBLANES = 8
 MIB = 1024 * 1024
-TILE = 256
+TILE = 512
 in_vmem = pl.BlockSpec(memory_space=pltpu.VMEM)
 in_smem = pl.BlockSpec(memory_space=pltpu.SMEM)
 anywhere = pl.BlockSpec(memory_space=pl.ANY)
@@ -146,7 +146,7 @@
     return jnp.where(place < capacity, labels, -1)
 
 
-def sent_kernel(per_owner, capacity, start_ref, slot_ref, sum_ref, sent_ref, held):
+def sent_kernel(per_owner, capacity, start_ref, slot_ref, after_ref, sum_ref, sent_ref, held):
     owner_count, span, _ = sent_ref.shape
     held[...] = jnp.full(held.shape, -1, jnp.int32)
     slots = slot_ref[...]
@@ -161,7 +161,7 @@
             sum_ref[owner : owner + 1, block * LANES : (block + 1) * LANES] = labels[block : block + 1, :]
 
 
-def sent_labels(starts, slots, owner_count, per_owner, capacity):
+def sent_labels(starts, slots, owner_count, per_owner, capacity, after):
     span = round_up(-(-capacity // LANES) + 1, SUBLANES)
     return pl.pallas_call(
         functools.partial(sent_kernel, per_owner, capacity),
@@ -169,12 +169,12 @@
             jax.ShapeDtypeStruct((owner_count, round_up(capacity + SUBLANES, LANES)), jnp.int32),
             jax.ShapeDtypeStruct((owner_count, span, LANES), jnp.int32),
         ),
-        in_specs=[in_smem, in_vmem],
+        in_specs=[in_smem, in_vmem, anywhere],
         out_specs=(in_vmem, in_vmem),
         scratch_shapes=[pltpu.VMEM((slots.shape[0] + 2 * SUBLANES, LANES), jnp.int32)],
         compiler_params=params(),
         name="sent",
-    )(starts, slots)
+    )(starts, slots, after)
 
 
 def arrived_kernel(blocks, turns_of, me_ref, got_ref, row_ref, column_ref, tally_ref):
@@ -277,17 +277,18 @@
         centroid_ref, me_ref, result_ref, *refs, out_ref, cosine_ref = refs
     else:
         out_ref, flat_ref, *refs = refs
-    mine, labels, tiles, even, odd, best, sem, tile_sem = refs
+    mine, turned, labels, tiles, even, odd, best, sem, tile_sem = refs
     first = begin // LANES
-    count = round_up(-(-begin // TILE), 2)
+    size = tiles.shape[2]
+    count = round_up(-(-begin // size), 2)
 
     def line_of(tile):
-        return jnp.minimum(tile * (TILE // LANES), first - TILE // LANES)
+        return jnp.minimum(tile * (size // LANES), first - size // LANES)
 
     def fetch(tile):
         start = pl.multiple_of(line_of(tile) * LANES, LANES)
         slot = lax.rem(tile, 4)
-        return pltpu.make_async_copy(flat_ref.at[pl.ds(start, TILE), :], tiles.at[slot], tile_sem.at[slot])
+        return pltpu.make_async_copy(flat_ref.at[:, pl.ds(start, size)], tiles.at[slot], tile_sem.at[slot])
 
     chunk_copy = pltpu.make_async_copy(chunk_ref, mine.at[pl.ds(0, rows), :], sem.at[0])
     label_copy = pltpu.make_async_copy(column_ref.at[pl.ds(begin, wide), :], labels, sem.at[1])
@@ -304,14 +305,13 @@
     best[...] = jnp.full(best.shape, -2.0, jnp.float32)
     chunk_copy.wait()
     label_copy.wait()
+    turned[...] = mine[:wide, :].T
     if not turns_of:
-        flat_copy = pltpu.make_async_copy(
-            mine.at[pl.ds(0, wide), :], flat_ref.at[pl.ds(begin, wide), :], sem.at[2]
-        )
+        flat_copy = pltpu.make_async_copy(turned, flat_ref.at[:, pl.ds(begin, wide)], sem.at[2])
         flat_copy.start()
 
     def products(right):
-        return lax.dot_general(mine[...], right, (((1,), (1,)), ((), ())), preferred_element_type=jnp.float32)
+        return jnp.dot(mine[...], right, preferred_element_type=jnp.float32)
 
     def cosines(values, line):
         cluster = lax.broadcasted_iota(jnp.int32, values.shape, 0)
@@ -319,7 +319,7 @@
         cosine_ref[pl.ds(line, 1), :] = jnp.sum(own, 0, keepdims=True)
 
     def reduce_tile(held, tile):
-        for part in range(TILE // LANES):
+        for part in range(size // LANES):
             line = line_of(tile) + part
             here = slice(part * LANES, (part + 1) * LANES)
             near = jnp.where(labels[...] == row_ref[pl.ds(line, 1), :], held[:wide, here], -2.0)
@@ -355,7 +355,7 @@
         odd[...] = products(tiles[(count - 1) % 4])
         reduce_tile(even, jnp.int32(count - 2))
         reduce_tile(odd, jnp.int32(count - 1))
-    own = products(mine[:wide, :])
+    own = products(turned[...])
     row = lax.broadcasted_iota(jnp.int32, (wide, LANES), 0)
     column = lax.broadcasted_iota(jnp.int32, (wide, LANES), 1)
     for block in range(wide // LANES):
@@ -384,7 +384,8 @@
     length, width = chunk.shape
     wide = round_up(length, LANES)
     tall = wide
-    flat_shape = jax.ShapeDtypeStruct((columns.shape[0], width), jnp.bfloat16)
+    size = min(TILE, begin) if begin else LANES
+    flat_shape = jax.ShapeDtypeStruct((width, columns.shape[0]), jnp.bfloat16)
     inputs = [chunk, rows, columns, best]
     in_specs = [anywhere, in_vmem, anywhere, in_vmem]
     aliases = {}
@@ -415,10 +416,11 @@
         out_specs=out_specs,
         scratch_shapes=[
             pltpu.VMEM((tall, width), jnp.bfloat16),
+            pltpu.VMEM((width, wide), jnp.bfloat16),
             pltpu.VMEM((wide, LANES), jnp.int32),
-            pltpu.VMEM((4, TILE, width), jnp.bfloat16),
-            pltpu.VMEM((tall, TILE), jnp.float32),
-            pltpu.VMEM((tall, TILE), jnp.float32),
+            pltpu.VMEM((4, width, size), jnp.bfloat16),
+            pltpu.VMEM((tall, size), jnp.float32),
+            pltpu.VMEM((tall, size), jnp.float32),
             pltpu.VMEM((wide, LANES), jnp.float32),
             pltpu.SemaphoreType.DMA((3,)),
             pltpu.SemaphoreType.DMA((4,)),
@@ -522,9 +524,6 @@
     return order[:1] + order[3:4] + order[1:3] + order[4:]
 
 
-IN_FLIGHT = 2
-
-
 def per_device(embeddings, assign, cluster_slot):
     row_count, width = embeddings.shape
     owner_count = lax.axis_size("docs")
@@ -535,57 +534,37 @@
     me = lax.axis_index("docs").astype(jnp.int32).reshape(1)
     turns_of = turns(owner_count)
 
-    pieces = []
-    for place, turn in enumerate(turns_of):
-        if capacity < padded or blocks < 5 or place < owner_count - 3:
-            cuts = [0, capacity]
-        elif place < owner_count - 1:
-            cuts = [0, 3 * LANES, capacity]
-        else:
-            cuts = [0, 2 * LANES, 4 * LANES, capacity]
-        for low, high in zip(cuts, cuts[1:]):
-            pieces.append((turn, low, high - low, place * padded + low))
-
     slots, starts = make_plan(
         assign.reshape(-1, LANES), cluster_slot.reshape(-1, LANES), owner_count, per_owner, row_count - capacity
     )
-    sum_labels, wire_labels = sent_labels(starts, slots, owner_count, per_owner, capacity)
-    got_labels = lax.all_to_all(wire_labels, "docs", split_axis=0, concat_axis=0, tiled=True)
-    rows, columns, group_tally = arrived_labels(me, got_labels, turns_of, blocks, width)
-
-    chunks, sent = [], []
-    bests = [jnp.full((owner_count * blocks, LANES), -2.0, jnp.float32)]
-    flat = group_share = share = None
-
-    def multiply(index):
-        after = [group_share] if index == len(pieces) // 4 else []
-        best, held = gram_step(rows, columns, bests[-1], flat, chunks[index], pieces[index][3], after)
-        bests.append(best)
-        return held
-
-    for index, (turn, offset, length, _) in enumerate(pieces):
-        after = [got_labels] if index == IN_FLIGHT else []
-        if index > IN_FLIGHT:
-            after += [chunks[index - IN_FLIGHT - (index == len(pieces) - 1)], sent[-1]]
-        if index > IN_FLIGHT + 2:
-            flat = multiply(index - IN_FLIGHT - 3)
-            after.append(bests[-1])
-        piece = unit_piece(starts, me, embeddings, turn, offset, length, after)
+
+    sent, chunks = [], []
+    for place, turn in enumerate(turns_of):
+        piece = unit_piece(starts, me, embeddings, turn, 0, capacity, sent[-1:] if place > 1 else [])
+        if place == 2:
+            sum_labels, wire_labels = sent_labels(starts, slots, owner_count, per_owner, capacity, sent[1])
+            got_labels = lax.all_to_all(wire_labels, "docs", split_axis=0, concat_axis=0, tiled=True)
+            piece = hold_until(piece, [got_labels])
         sent.append(piece)
         if turn:
             piece = lax.ppermute(piece, "docs", [(i, (i + turn) % owner_count) for i in range(owner_count)])
         chunks.append(piece)
-        if index == IN_FLIGHT + 1:
-            partial_sums = slot_sums(starts, sum_labels, embeddings, per_owner, capacity, sent[: IN_FLIGHT + 1])
-            partial_sums = hold_until(partial_sums, chunks[1 : IN_FLIGHT + 1] + sent[IN_FLIGHT + 1 :])
-            group_share = lax.psum_scatter(partial_sums, "grp", scatter_dimension=1, tiled=True)
-            share = lax.psum_scatter(group_share, "docs", scatter_dimension=0, tiled=True)[0]
-    for index in range(len(bests) - 1, len(pieces) - 1):
-        flat = multiply(index)
-    packed = pack_share(share, group_tally, [bests[-2], sent[-1]])
+    rows, columns, group_tally = arrived_labels(me, got_labels, turns_of, blocks, width)
+    partial_sums = slot_sums(starts, sum_labels, embeddings, per_owner, capacity, sent[1:5])
+    partial_sums = hold_until(partial_sums, chunks[1:3])
+    group_share = lax.psum_scatter(partial_sums, "grp", scatter_dimension=1, tiled=True)
+    share = lax.psum_scatter(group_share, "docs", scatter_dimension=0, tiled=True)[0]
+
+    bests = [jnp.full((owner_count * blocks, LANES), -2.0, jnp.float32)]
+    flat = None
+    for place in range(owner_count - 1):
+        after = [group_share] if place == 2 else []
+        best, flat = gram_step(rows, columns, bests[-1], flat, chunks[place], place * padded, after)
+        bests.append(best)
+    packed = pack_share(share, group_tally, bests[-3:-2])
     centroids, centroid_unit = make_centroids(lax.all_gather(packed, "grp"), per_owner)
     results = gram_step(
-        rows, columns, bests[-1], flat, chunks[-1], pieces[-1][3], final=(centroid_unit, me, turns_of)
+        rows, columns, bests[-1], flat, chunks[-1], (owner_count - 1) * padded, final=(centroid_unit, me, turns_of)
     )
     back = lax.all_to_all(results, "docs", split_axis=0, concat_axis=0, tiled=True)
     near, cosine = place_rows(starts, slots, back, per_owner)

time: 346 us -> 355 us (1.026); the launches traced: 344 us -> 349 us
  waiting for transfers between devices: 70 us -> 175 us
  Pallas kernels: 161 us -> 111 us
  starting transfers between devices: 49.8 us -> 14.9 us
  blocking collectives: 41.3 us -> 27.2 us
    ppermute x11 -> x7, waiting for transfers between devices: 69.8 us -> 131 us  [per_device(): lax.ppermute(piece, 'docs', [(i, (i + turn) % owner_count) for i in range...]
    pallas_call x12 -> x8, Pallas kernels: 113 us -> 67.6 us  [gram_step(): pl.pallas_call(functools.partial(gram_kernel, begin, length, wide, len(af...]
    reduce_scatter x1, waiting for transfers between devices: 0.01 us -> 42.7 us  [per_device(): lax.psum_scatter(partial_sums, 'grp', scatter_dimension=1, tiled=True)]
    ppermute x11 -> x7, starting transfers between devices: 43.4 us -> 8.48 us  [per_device(): lax.ppermute(piece, 'docs', [(i, (i + turn) % owner_count) for i in range...]
    all_to_all x1, blocking collectives: 31.2 us -> 17.2 us  [per_device(): lax.all_to_all(results, 'docs', split_axis=0, concat_axis=0, tiled=True)]
    pallas_call x12 -> x8, Pallas kernels: 28.1 us -> 23.1 us  [unit_piece(): pl.pallas_call(functools.partial(unit_kernel, steps, offset, turn), out_s...]
    unnamed x32 -> x16, local copies, waits for them, and re-layouts: 7.18 us -> 6.92 us
  transfers between devices with their start and end apart: 14 -> 10, of which waited for: 7 -> 8; matrix products, arithmetic and copies ran while one was open for 0% -> 0% of each run, Pallas kernels for 42% -> 26%
where the time goes in v1:
time: 355 us; the launch traced here: 349 us
  waiting for transfers between devices  175 us (49%)
  Pallas kernels  111 us (31%)
  blocking collectives  27.2 us (8%)
  starting transfers between devices  14.9 us (4%)
  between operations  14.7 us (4%)
  local copies, waits for them, and re-layouts  6.92 us (2%)
    ppermute x7, waiting for transfers between devices, per_device(): lax.ppermute(piece, 'docs', [(i, (i + turn) % owner_count) for i in range...  131 us
    pallas_call x8, Pallas kernels, gram_step(): pl.pallas_call(functools.partial(gram_kernel, begin, length, wide, len(af...  67.6 us
    reduce_scatter x1, waiting for transfers between devices, per_device(): lax.psum_scatter(partial_sums, 'grp', scatter_dimension=1, tiled=True)  42.7 us
    pallas_call x8, Pallas kernels, unit_piece(): pl.pallas_call(functools.partial(unit_kernel, steps, offset, turn), out_s...  23.1 us
    all_to_all x1, blocking collectives, per_device(): lax.all_to_all(results, 'docs', split_axis=0, concat_axis=0, tiled=True)  17.2 us
    pallas_call x1, Pallas kernels, slot_sums(): pl.pallas_call(sum_kernel, out_shape=jax.ShapeDtypeStruct((owner_count, p...  14.9 us
    all_gather x1, blocking collectives, per_device(): lax.all_gather(packed, 'grp')  9.99 us
    ppermute x7, starting transfers between devices, per_device(): lax.ppermute(piece, 'docs', [(i, (i + turn) % owner_count) for i in range...  8.48 us
  transfers between devices with their start and end apart: 10, of which 8 were waited for; matrix products, arithmetic and copies ran while one was open for 0% of the time, Pallas kernels for 26%

profile of v1, /device:TPU:0, one launch (start us, length us, event | category | flops | bytes accessed | tf_op | source)
XLA Modules:
  0.0 349.3 jit_solution(460669871955059144)
XLA Ops:
  13.3 6.3 %all-to-all-start = ((s32[8,8,128]{2,1,0:T(8,128)}), s32[8,8,128]{2,1,0:T(8,128)S(1)}, u32[]{:S(2)}, u32[]{:S(2)}) async-start(s32[8,8,128]{2,1,0:T(8,128)} %get-tuple-element.31), calls=%async_computation | async-start | bytes 65536 | tf_op jit(solution)/shard_map/all_to_all | solution.py:546
  25.4 3.6 %unit.10.refs_0_.refs_2_ = bf16[640,1024]{1,0:T(8,128)(2,1)} custom-call(s32[8]{0:T(128)S(1)} %get-tuple-element.28.start_ref, s32[1]{0:T(128)} %bitcast.2.me_ref.refs_6_, f32[4096,1024]{1,0:T(8,128)} %rows_ref.17, bf16[640,1024]{1,0:T(8,128)(2,1)S(1)} %hold.2.refs_0_.refs_1_), custom_call_target="tpu_custom_call" | custom-call | flops 1000 | bytes 1000 | tf_op jit(solution)/shard_map/unit/pallas_call | solution.py:93
  29.0 3.5 %unit.11.refs_3_.refs_0_ = bf16[640,1024]{1,0:T(8,128)(2,1)} custom-call(s32[8]{0:T(128)S(1)} %get-tuple-element.28.start_ref, s32[1]{0:T(128)} %bitcast.2.me_ref.refs_6_, f32[4096,1024]{1,0:T(8,128)} %rows_ref.17, bf16[640,1024]{1,0:T(8,128)(2,1)} %unit.10.refs_0_.refs_2_), custom_call_target="tpu_custom_call" | custom-call | flops 1000 | bytes 1000 | tf_op jit(solution)/shard_map/unit/pallas_call | solution.py:93
  32.6 14.9 %sums.1.refs_0_ = f32[8,96,1024]{2,1,0:T(8,128)} custom-call(s32[8]{0:T(128)S(1)} %get-tuple-element.28.start_ref, s32[8,768]{1,0:T(8,128)S(1)} %get-tuple-element.30.label_ref, f32[4096,1024]{1,0:T(8,128)} %rows_ref.17, bf16[640,1024]{1,0:T(8,128)(2,1)S(1)} %unit.8.after_ref.refs_0_, bf16[640,1024]{1,0:T(8,128)(2,1)S(1)} %hold.2.refs_0_.refs_1_, ...), custom_call_target="tpu_custom_call" | custom-call | flops 3019898880 | bytes 16777216 | tf_op jit(solution)/shard_map/sums/pallas_call | solution.py:251
  47.5 6.3 %collective-permute-done.refs_1_.refs_0_ = bf16[640,1024]{1,0:T(8,128)(2,1)} collective-permute-done((bf16[640,1024]{1,0:T(8,128)(2,1)S(1)}, bf16[640,1024]{1,0:T(8,128)(2,1)}, u32[]{:S(2)}, u32[]{:S(2)}) %collective-permute-start) | collective-permute-done | bytes 1310752 | tf_op jit(solution)/shard_map/ppermute | solution.py:550
  53.8 13.5 %collective-permute-done.1.refs_2_.refs_0_ = bf16[640,1024]{1,0:T(8,128)(2,1)S(1)} collective-permute-done((bf16[640,1024]{1,0:T(8,128)(2,1)S(1)}, bf16[640,1024]{1,0:T(8,128)(2,1)S(1)}, u32[]{:S(2)}, u32[]{:S(2)}) %collective-permute-start.1) | collective-permute-done | bytes 1310752 | tf_op jit(solution)/shard_map/ppermute | solution.py:550
  72.0 42.7 %reduce-scatter.3.cloned.1.call-done.refs_5_ = f32[8,24,1024]{2,1,0:T(8,128)} async-done(((f32[8,96,1024]{2,1,0:T(8,128)}), f32[8,24,1024]{2,1,0:T(8,128)}) %reduce-scatter.3.cloned.1.call-update) | async-done | bytes 786448 | tf_op jit(solution)/shard_map/reduce_scatter | solution.py:555
  114.7 2.8 collective-permute-start.3
  120.7 2.5 unit.14.refs_0_
  123.3 2.9 collective-permute-start.5
  126.1 3.5 %unit.15 = bf16[640,1024]{1,0:T(8,128)(2,1)} custom-call(s32[8]{0:T(128)S(1)} %get-tuple-element.28.start_ref, s32[1]{0:T(128)} %bitcast.2.me_ref.refs_6_, f32[4096,1024]{1,0:T(8,128)} %rows_ref.17, bf16[640,1024]{1,0:T(8,128)(2,1)S(1)} %unit.14.refs_0_), custom_call_target="tpu_custom_call" | custom-call | flops 1000 | bytes 1000 | tf_op jit(solution)/shard_map/unit/pallas_call | solution.py:93
  135.6 5.5 %gram.9 = (f32[40,128]{1,0:T(8,128)S(1)}, bf16[1024,5120]{1,0:T(8,128)(2,1)}) custom-call(bf16[640,1024]{1,0:T(8,128)(2,1)} %collective-permute-done.refs_1_.refs_0_, s32[40,128]{1,0:T(8,128)S(1)} %get-tuple-element.33.refs_1_, s32[5120,128]{1,0:T(8,128)S(1)} %get-tuple-element.34.refs_2_, ...), custom_call_target="tpu_custom_call", output_to_operand_aliasing={{1}: (4, {})} | custom-call | flops 1000 | bytes 1000 | tf_op jit(solution)/shard_map/gram/pallas_call | solution.py:412
  141.1 7.2 %gram.10 = (f32[40,128]{1,0:T(8,128)S(1)}, bf16[1024,5120]{1,0:T(8,128)(2,1)}) custom-call(bf16[640,1024]{1,0:T(8,128)(2,1)S(1)} %copy-done.3, s32[40,128]{1,0:T(8,128)S(1)} %get-tuple-element.33.refs_1_, s32[5120,128]{1,0:T(8,128)S(1)} %get-tuple-element.34.refs_2_, f32[40,128]{1,0:T(8,128)S(1)} %get-tuple-element.37.refs_3_, ...), custom_call_target="tpu_custom_call", output_to_operand_aliasing={{1}: (4, {})} | custom-call | flops 1000 | bytes 1000 | tf_op jit(solution)/shard_map/gram/pallas_call | solution.py:412
  148.3 3.4 collective-permute-done.3.refs_0_
  151.7 7.4 %gram.11 = (f32[40,128]{1,0:T(8,128)S(1)}, bf16[1024,5120]{1,0:T(8,128)(2,1)}) custom-call(bf16[640,1024]{1,0:T(8,128)(2,1)S(1)} %collective-permute-done.3.refs_0_, s32[40,128]{1,0:T(8,128)S(1)} %get-tuple-element.33.refs_1_, s32[5120,128]{1,0:T(8,128)S(1)} %get-tuple-element.34.refs_2_, ...), custom_call_target="tpu_custom_call", output_to_operand_aliasing={{1}: (4, {})} | custom-call | flops 1000 | bytes 1000 | tf_op jit(solution)/shard_map/gram/pallas_call | solution.py:412
  159.1 46.4 %collective-permute-done.2.refs_0_ = bf16[640,1024]{1,0:T(8,128)(2,1)S(1)} collective-permute-done((bf16[640,1024]{1,0:T(8,128)(2,1)}, bf16[640,1024]{1,0:T(8,128)(2,1)S(1)}, u32[]{:S(2)}, u32[]{:S(2)}) %collective-permute-start.2) | collective-permute-done | bytes 1310752 | tf_op jit(solution)/shard_map/ppermute | solution.py:550
  205.5 8.6 %gram.12 = (f32[40,128]{1,0:T(8,128)S(1)}, bf16[1024,5120]{1,0:T(8,128)(2,1)}) custom-call(bf16[640,1024]{1,0:T(8,128)(2,1)S(1)} %collective-permute-done.2.refs_0_, s32[40,128]{1,0:T(8,128)S(1)} %get-tuple-element.33.refs_1_, s32[5120,128]{1,0:T(8,128)S(1)} %get-tuple-element.34.refs_2_, ...), custom_call_target="tpu_custom_call", output_to_operand_aliasing={{1}: (4, {})} | custom-call | flops 1000 | bytes 1000 | tf_op jit(solution)/shard_map/gram/pallas_call | solution.py:412
  214.2 11.1 %gram.13 = (f32[40,128]{1,0:T(8,128)S(1)}, bf16[1024,5120]{1,0:T(8,128)(2,1)}) custom-call(bf16[640,1024]{1,0:T(8,128)(2,1)S(1)} %collective-permute-done.6.refs_0_, s32[40,128]{1,0:T(8,128)S(1)} %get-tuple-element.33.refs_1_, s32[5120,128]{1,0:T(8,128)S(1)} %get-tuple-element.34.refs_2_, ...), custom_call_target="tpu_custom_call", output_to_operand_aliasing={{1}: (4, {})} | custom-call | flops 1000 | bytes 1000 | tf_op jit(solution)/shard_map/gram/pallas_call | solution.py:412
  225.3 13.3 %collective-permute-done.5.refs_0_ = bf16[640,1024]{1,0:T(8,128)(2,1)S(1)} collective-permute-done((bf16[640,1024]{1,0:T(8,128)(2,1)S(1)}, bf16[640,1024]{1,0:T(8,128)(2,1)S(1)}, u32[]{:S(2)}, u32[]{:S(2)}) %collective-permute-start.5) | collective-permute-done | bytes 1310752 | tf_op jit(solution)/shard_map/ppermute | solution.py:550
  238.5 10.9 %gram.14 = (f32[40,128]{1,0:T(8,128)S(1)}, bf16[1024,5120]{1,0:T(8,128)(2,1)}) custom-call(bf16[640,1024]{1,0:T(8,128)(2,1)S(1)} %collective-permute-done.5.refs_0_, s32[40,128]{1,0:T(8,128)S(1)} %get-tuple-element.33.refs_1_, s32[5120,128]{1,0:T(8,128)S(1)} %get-tuple-element.34.refs_2_, ...), custom_call_target="tpu_custom_call", output_to_operand_aliasing={{1}: (4, {})} | custom-call | flops 1000 | bytes 1000 | tf_op jit(solution)/shard_map/gram/pallas_call | solution.py:412
  250.3 10.0 %all-gather = f32[128,1024]{1,0:T(8,128)S(1)} all-gather(f32[32,1024]{1,0:T(8,128)S(1)} %pack.1), channel_id=2, replica_groups=mesh['grp'=4,'docs'=8] {'grp'}, dimensions={0}, use_global_device_ids=true | all-gather | bytes 655360 | tf_op jit(solution)/shard_map/all_gather | solution.py:565
  261.2 47.7 %collective-permute-done.4.refs_0_ = bf16[640,1024]{1,0:T(8,128)(2,1)} collective-permute-done((bf16[640,1024]{1,0:T(8,128)(2,1)}, bf16[640,1024]{1,0:T(8,128)(2,1)}, u32[]{:S(2)}, u32[]{:S(2)}) %collective-permute-start.4) | collective-permute-done | bytes 1310752 | tf_op jit(solution)/shard_map/ppermute | solution.py:550
  308.9 14.6 %gram.15 = f32[8,16,128]{2,1,0:T(8,128)S(1)} custom-call(bf16[640,1024]{1,0:T(8,128)(2,1)} %collective-permute-done.4.refs_0_, s32[40,128]{1,0:T(8,128)S(1)} %get-tuple-element.33.refs_1_, s32[5120,128]{1,0:T(8,128)S(1)} %get-tuple-element.34.refs_2_, f32[40,128]{1,0:T(8,128)S(1)} %get-tuple-element.48.refs_3_, ...), custom_call_target="tpu_custom_call" | custom-call | flops 1000 | bytes 1000 | tf_op jit(solution)/shard_map/gram/pallas_call | solution.py:412
  323.5 17.2 %all_to_all.10.back_ref = f32[8,16,128]{2,1,0:T(8,128)S(1)} all-to-all(f32[8,16,128]{2,1,0:T(8,128)S(1)} %gram.15), channel_id=1, replica_groups=mesh['grp'=4,'docs'=8] {'docs'}, dimensions={0} | all-to-all | bytes 131072 | tf_op jit(solution)/shard_map/all_to_all | solution.py:569
  (42 shorter events, 28.7 us)
Async XLA Ops:
  7.2 0.7 copy-start.6
  7.9 0.7 copy-start.7
  13.3 12.2 %all-to-all-start = ((s32[8,8,128]{2,1,0:T(8,128)}), s32[8,8,128]{2,1,0:T(8,128)S(1)}, u32[]{:S(2)}, u32[]{:S(2)}) async-start(s32[8,8,128]{2,1,0:T(8,128)} %get-tuple-element.31), calls=%async_computation | async-start | bytes 65536 | tf_op jit(solution)/shard_map/all_to_all | solution.py:546
  19.6 95.1 %reduce-scatter.3.cloned.1.call-start = ((), (), s32[]{:S(2)}) async-start(), calls=%async_computation.4 | async-start | bytes 3932160 | tf_op jit(solution)/shard_map/reduce_scatter | solution.py:555
  19.6 34.2 %collective-permute-start = (bf16[640,1024]{1,0:T(8,128)(2,1)S(1)}, bf16[640,1024]{1,0:T(8,128)(2,1)}, u32[]{:S(2)}, u32[]{:S(2)}) collective-permute-start(bf16[640,1024]{1,0:T(8,128)(2,1)S(1)} %unit.8.after_ref.refs_0_), channel_id=1, source_target_pairs={{0,2},{1,3},{2,4},{3,5},{4,6},{5,7},{6,0},{7,1},{8,10},{9,11},{10,... | collective-permute-start | bytes 3932168 | tf_op jit(solution)/shard_map/ppermute | solution.py:550
  25.4 41.8 %collective-permute-start.1 = (bf16[640,1024]{1,0:T(8,128)(2,1)S(1)}, bf16[640,1024]{1,0:T(8,128)(2,1)S(1)}, u32[]{:S(2)}, u32[]{:S(2)}) collective-permute-start(bf16[640,1024]{1,0:T(8,128)(2,1)S(1)} %hold.2.refs_0_.refs_1_), channel_id=1, source_target_pairs={{0,1},{1,2},{2,3},{3,4},{4,5},{5,6},{6,7},{7,0},{8,9},{9,10},{10,1... | collective-permute-start | bytes 3932168 | tf_op jit(solution)/shard_map/ppermute | solution.py:550
  67.3 1.9 copy-start
  69.2 1.6 copy-start.1
  70.8 1.1 copy-start.2
  71.9 177.5 %reduce-scatter.5.cloned.1.call-start = ((), (), s32[]{:S(2)}) async-start(), calls=%async_computation.5 | async-start | bytes 884736 | tf_op jit(solution)/shard_map/reduce_scatter | solution.py:556
  114.7 37.0 %collective-permute-start.3 = (bf16[640,1024]{1,0:T(8,128)(2,1)}, bf16[640,1024]{1,0:T(8,128)(2,1)S(1)}, u32[]{:S(2)}, u32[]{:S(2)}) collective-permute-start(bf16[640,1024]{1,0:T(8,128)(2,1)} %unit.10.refs_0_.refs_2_), channel_id=1, source_target_pairs={{0,7},{1,0},{2,1},{3,2},{4,3},{5,4},{6,5},{7,6},{8,15},{9,8},{10,9... | collective-permute-start | bytes 3932168 | tf_op jit(solution)/shard_map/ppermute | solution.py:550
  117.5 88.0 %collective-permute-start.2 = (bf16[640,1024]{1,0:T(8,128)(2,1)}, bf16[640,1024]{1,0:T(8,128)(2,1)S(1)}, u32[]{:S(2)}, u32[]{:S(2)}) collective-permute-start(bf16[640,1024]{1,0:T(8,128)(2,1)} %unit.11.refs_3_.refs_0_), channel_id=1, source_target_pairs={{0,6},{1,7},{2,0},{3,1},{4,2},{5,3},{6,4},{7,5},{8,14},{9,15},{10,... | collective-permute-start | bytes 3932168 | tf_op jit(solution)/shard_map/ppermute | solution.py:550
  120.7 93.5 %collective-permute-start.6 = (bf16[640,1024]{1,0:T(8,128)(2,1)S(1)}, bf16[640,1024]{1,0:T(8,128)(2,1)S(1)}, u32[]{:S(2)}, u32[]{:S(2)}) collective-permute-start(bf16[640,1024]{1,0:T(8,128)(2,1)S(1)} %unit.13.refs_0_), channel_id=1, source_target_pairs={{0,3},{1,4},{2,5},{3,6},{4,7},{5,0},{6,1},{7,2},{8,11},{9,12},{10,... | collective-permute-start | bytes 3932168 | tf_op jit(solution)/shard_map/ppermute | solution.py:550
  123.3 115.2 %collective-permute-start.5 = (bf16[640,1024]{1,0:T(8,128)(2,1)S(1)}, bf16[640,1024]{1,0:T(8,128)(2,1)S(1)}, u32[]{:S(2)}, u32[]{:S(2)}) collective-permute-start(bf16[640,1024]{1,0:T(8,128)(2,1)S(1)} %unit.14.refs_0_), channel_id=1, source_target_pairs={{0,5},{1,6},{2,7},{3,0},{4,1},{5,2},{6,3},{7,4},{8,13},{9,14},{10,... | collective-permute-start | bytes 3932168 | tf_op jit(solution)/shard_map/ppermute | solution.py:550
  129.7 179.2 %collective-permute-start.4 = (bf16[640,1024]{1,0:T(8,128)(2,1)}, bf16[640,1024]{1,0:T(8,128)(2,1)}, u32[]{:S(2)}, u32[]{:S(2)}) collective-permute-start(bf16[640,1024]{1,0:T(8,128)(2,1)} %unit.15), channel_id=1, source_target_pairs={{0,4},{1,5},{2,6},{3,7},{4,0},{5,1},{6,2},{7,3},{8,12},{9,13},{10,... | collective-permute-start | bytes 3932168 | tf_op jit(solution)/shard_map/ppermute | solution.py:550
  135.6 5.5 %copy-start.3 = (bf16[640,1024]{1,0:T(8,128)(2,1)S(1)}, bf16[640,1024]{1,0:T(8,128)(2,1)}, u32[]{:S(2)}) copy-start(bf16[640,1024]{1,0:T(8,128)(2,1)} %copy-done.2) | copy-start | bytes 3932164
  135.6 5.5 %copy-start.4 = (f32[8,24,1024]{2,1,0:T(8,128)S(1)}, f32[8,24,1024]{2,1,0:T(8,128)}, u32[]{:S(2)}) copy-start(f32[8,24,1024]{2,1,0:T(8,128)} %reduce-scatter.3.cloned.1.call-done.refs_5_) | copy-start | bytes 2359300
  249.4 0.9 copy-start.5
Sparse Core Ops, SparseCore 0:
  72.0 42.6 reduce-scatter.2
  117.0 81.8 reduce-scatter.4
